TPU v7x, 32 devices: a whole 2x2x4 slice. The times are simulated.
32 devices in a mesh: groups: 2 (over y), blk: 8 (over z, x), mp: 2 (over core).
Axes of the slice: x: 2, y: 2, z: 4, core: 2. Of those that a mesh axis runs over, the one named last changes fastest.
Arguments:
- probe_vectors: bfloat16 [12, 8, 32, 3584], P('groups', 'blk', None, 'mp'), parts along dimension 0, may hold values from -12 to 12
- unsettled_lookups: bfloat16 [12, 8, 32, 512], P('groups', 'blk', None, 'mp'), parts along dimension 0, may hold values from -6 to 6
- unsettled_payloads: bfloat16 [12, 8, 32, 512], P('groups', 'blk', None, 'mp'), parts along dimension 0, may hold values from -6 to 6
- uncover_ordering: int32 [12, 8, 32], P('groups', 'blk'), parts along dimension 0, may hold values from 0 to 31, each once within a row
- rounds_finished: int32 [12, 8], P('groups', 'blk'), parts along dimension 0, may hold values from 0 to 7
- random_entry_choice: int32 [12, 8, 32], P('groups', 'blk'), parts along dimension 0, may hold values from 0 to 63
- noise_token_keys: bfloat16 [64, 512], P(None, 'mp'), may hold values from -6 to 6
- noise_token_values: bfloat16 [64, 512], P(None, 'mp'), may hold values from -6 to 6
- prefix_key_cache: bfloat16 [2, 8, 32, 512], P('groups', 'blk', None, 'mp'), parts along dimension 0, may hold values from -6 to 6
- prefix_value_cache: bfloat16 [2, 8, 32, 512], P('groups', 'blk', None, 'mp'), parts along dimension 0, may hold values from -6 to 6
- completed_keys: bfloat16 [16, 32, 512], P(('groups', 'blk'), None, 'mp'), parts along dimension 0, may hold values from -6 to 6
- completed_values: bfloat16 [16, 32, 512], P(('groups', 'blk'), None, 'mp'), parts along dimension 0, may hold values from -6 to 6
- committing_index: int32 [2], P('groups'), parts along dimension 0, may hold values from 0 to 7, as said below
Outputs:
- attended: bfloat16 [12, 8, 32, 3584], P('groups', 'blk', None, 'mp'), parts along dimension 0
There are 2 independent parts, one for each index of `groups`. A program takes and returns all parts, laid end to end along the dimension named above; an argument that names none is the same for every part. Nothing has to cross between parts.
Inputs may be any that keep to these rules, and one draw needn't show every extreme that they name: `committing_index`: an index of blk; in every odd part it is the last index, 7.
All inputs are finite; a program needn't handle non-finite values.
Results may differ from a plain program's by a relative error of at most 0.005.
Values may be sent and summed in bfloat16 or wider, within the bound.
A program may use at most 128 MiB of HBM per device.

v0:
```python
import jax
import jax.numpy as jnp
from jax import lax
from jax.sharding import PartitionSpec as P

QUERY_GROUPS = 28
MEMORY_GROUPS = 4
FEATURE_DIM = 128
UNMASK = 4


def shifted(block, axis, distance):
    devices = range(lax.axis_size(axis))
    route = [((i - distance) % len(devices), i) for i in devices]
    return lax.ppermute(block, axis, route)


def arrange(tensor, heads):
    return jnp.transpose(tensor.reshape(-1, heads, FEATURE_DIM), (1, 0, 2))


def absorb(carry, score, values, form):
    top, total, summed = carry
    newtop = jnp.maximum(top, jnp.max(score, axis=-1))
    factor = jnp.exp(top - newtop)
    weight = jnp.exp(score - newtop[..., None])
    total = total * factor + jnp.sum(weight, axis=-1)
    part = jnp.einsum(form, weight.astype(jnp.bfloat16), values, preferred_element_type=jnp.float32)
    return (newtop, total, summed * factor[..., None] + part)


def on_device(
    probe_vectors,
    unsettled_lookups,
    unsettled_payloads,
    uncover_ordering,
    rounds_finished,
    random_entry_choice,
    noise_token_keys,
    noise_token_values,
    prefix_key_cache,
    prefix_value_cache,
    completed_keys,
    completed_values,
    committing_index,
):
    slots = probe_vectors.shape[0]
    block = probe_vectors.shape[2]
    reveal_width = noise_token_keys.shape[1]
    heads = reveal_width // FEATURE_DIM
    group = QUERY_GROUPS // MEMORY_GROUPS
    scale = FEATURE_DIM ** (-0.5)
    rows = slots * block * group
    concealed_flags = uncover_ordering >= UNMASK * rounds_finished[:, :, None]
    onehot = (
        random_entry_choice[..., None] == jnp.arange(noise_token_keys.shape[0], dtype=jnp.int32)
    ).astype(jnp.bfloat16)
    table = jnp.concatenate([noise_token_keys, noise_token_values], axis=1)
    still_noised = jnp.dot(
        onehot.reshape(-1, noise_token_keys.shape[0]), table, preferred_element_type=jnp.float32
    ).astype(jnp.bfloat16)
    still_noised = still_noised.reshape(slots, 1, block, 2 * reveal_width)
    own_span_lookups = jnp.where(
        concealed_flags[..., None], still_noised[..., :reveal_width], unsettled_lookups
    )
    own_span_payloads = jnp.where(
        concealed_flags[..., None], still_noised[..., reveal_width:], unsettled_payloads
    )
    got_keys, got_values = shifted((own_span_lookups, own_span_payloads), "blk", 1)
    first = lax.axis_index("blk") == 0
    prev_keys = jnp.where(first, jnp.roll(got_keys, 1, axis=0), got_keys)
    prev_values = jnp.where(first, jnp.roll(got_values, 1, axis=0), got_values)
    owner = committing_index[0]
    mine = lax.axis_index("blk") == owner
    summed_keys, summed_values = lax.psum(
        (
            jnp.where(mine, completed_keys.astype(jnp.float32), 0.0),
            jnp.where(mine, completed_values.astype(jnp.float32), 0.0),
        ),
        "blk",
    )
    commit_keys = summed_keys.astype(jnp.bfloat16)
    commit_values = summed_values.astype(jnp.bfloat16)
    ordered = jnp.transpose(
        probe_vectors.reshape(slots, block, heads, group, FEATURE_DIM), (2, 0, 1, 3, 4)
    )
    shared_q = ordered.reshape(heads, rows, FEATURE_DIM)
    carry = (
        jnp.full((heads, rows), -1e30, jnp.float32),
        jnp.zeros((heads, rows), jnp.float32),
        jnp.zeros((heads, rows, FEATURE_DIM), jnp.float32),
    )

    def attend_shared(state, keys, values):
        score = (
            jnp.einsum("grd,gnd->grn", shared_q, keys, preferred_element_type=jnp.float32) * scale
        )
        return absorb(state, score, values, "grn,gnd->grd")

    whole_keys, whole_values = (
        lax.all_gather(prefix_key_cache, "blk", axis=1, tiled=True),
        lax.all_gather(prefix_value_cache, "blk", axis=1, tiled=True),
    )
    all_keys = arrange(whole_keys, heads)
    all_values = arrange(whole_values, heads)
    length = all_keys.shape[1]
    span = min(512, length)

    def one_span(position_number, state):
        start = position_number * span
        keys = lax.dynamic_slice_in_dim(all_keys, start, span, 1)
        values = lax.dynamic_slice_in_dim(all_values, start, span, 1)
        return attend_shared(state, keys, values)

    carry = lax.fori_loop(0, length // span, one_span, carry)
    carry = attend_shared(carry, arrange(commit_keys, heads), arrange(commit_values, heads))
    slot_q = shared_q.reshape(heads, slots, block * group, FEATURE_DIM)
    carry = (
        carry[0].reshape(heads, slots, block * group),
        carry[1].reshape(heads, slots, block * group),
        carry[2].reshape(heads, slots, block * group, FEATURE_DIM),
    )

    def attend_slots(state, keys, values):
        slot_keys = jnp.transpose(keys.reshape(slots, block, heads, FEATURE_DIM), (2, 0, 1, 3))
        slot_values = jnp.transpose(values.reshape(slots, block, heads, FEATURE_DIM), (2, 0, 1, 3))
        score = (
            jnp.einsum("gsrd,gsnd->gsrn", slot_q, slot_keys, preferred_element_type=jnp.float32)
            * scale
        )
        return absorb(state, score, slot_values, "gsrn,gsnd->gsrd")

    carry = attend_slots(carry, prev_keys, prev_values)
    carry = attend_slots(carry, own_span_lookups, own_span_payloads)
    attended_output = carry[2] / carry[1][..., None]
    attended_output = jnp.transpose(
        attended_output.reshape(heads, slots, block, group, FEATURE_DIM), (1, 2, 0, 3, 4)
    )
    attended_output = attended_output.reshape(slots, 1, block, heads * group * FEATURE_DIM)
    return jnp.where(concealed_flags[..., None], attended_output, 0.0).astype(jnp.bfloat16)


def solution(mesh):
    placed = (
        P("groups", "blk", None, "mp"),
        P("groups", "blk", None, "mp"),
        P("groups", "blk", None, "mp"),
        P("groups", "blk", None),
        P("groups", "blk"),
        P("groups", "blk", None),
        P(None, "mp"),
        P(None, "mp"),
        P("groups", "blk", None, "mp"),
        P("groups", "blk", None, "mp"),
        P(("groups", "blk"), None, "mp"),
        P(("groups", "blk"), None, "mp"),
        P("groups"),
    )
    return jax.shard_map(
        on_device,
        mesh=mesh,
        in_specs=placed,
        out_specs=P("groups", "blk", None, "mp"),
        check_vma=False,
    )
```

profile of v0, /device:TPU:0, one launch (start us, length us, event | category | flops | bytes accessed | tf_op | source)
XLA Modules:
  0.0 133.8 jit_solution(1054010733148320517)
XLA Ops:
  0.0 0.7 multiply_bitcast_fusion
  0.7 0.8 broadcast_compare_fusion
  1.5 0.7 reduce
  2.2 0.1 eq.26
  2.3 1.0 convolution_convert_fusion
  3.3 1.7 %slice_select_fusion = (bf16[6,1,32,256]{3,2,1,0:T(8,128)(2,1)}, bf16[6,1,32,256]{3,2,1,0:T(8,128)(2,1)S(1)}) fusion(bf16[6,1,32,256]{3,2,1,0:T(8,128)(2,1)} %param.15, bf16[6,1,32,512]{3,2,1,0:T(8,128)(2,1)S(1)} %bitcast.85, pred[6,32]{1,0:T(8,128)(4,1)S(1)} %bitcast.88, bf16[6,1,32,256]{3,2,1,0:T(8,128)(2,1)} %param.14), kind=kLoop, calls=%fused_computation.41 | loop fusion | flops 98304 | bytes 590016 | tf_op jit(solution)/shard_map/jit(_where)/select_n | solution.py:66
  5.0 2.9 %collective-permute-start.1 = (bf16[6,1,32,256]{3,2,1,0:T(8,128)(2,1)}, bf16[6,1,32,256]{3,2,1,0:T(8,128)(2,1)}, u32[]{:S(2)}, u32[]{:S(2)}) collective-permute-start(bf16[6,1,32,256]{3,2,1,0:T(8,128)(2,1)} %get-tuple-element.36), channel_id=1, source_target_pairs={{14,0},{0,2},{2,4},{4,6},{6,8},{8,10},{10,12},{12,14},{15,1},{1,3}... | collective-permute-start | bytes 294920 | tf_op jit(solution)/shard_map/ppermute | solution.py:15
  7.9 1.5 %collective-permute-start = (bf16[6,1,32,256]{3,2,1,0:T(8,128)(2,1)S(1)}, bf16[6,1,32,256]{3,2,1,0:T(8,128)(2,1)}, u32[]{:S(2)}, u32[]{:S(2)}) collective-permute-start(bf16[6,1,32,256]{3,2,1,0:T(8,128)(2,1)S(1)} %get-tuple-element.37), channel_id=1, source_target_pairs={{14,0},{0,2},{2,4},{4,6},{6,8},{8,10},{10,12},{12,14},{15,1},{1,3}... | collective-permute-start | bytes 294920 | tf_op jit(solution)/shard_map/ppermute | solution.py:15
  9.5 1.6 %reshape.205 = bf16[6,32,2,128]{3,2,1,0:T(2,128)(2,1)} reshape(bf16[6,1,32,256]{3,2,1,0:T(8,128)(2,1)} %get-tuple-element.36) | data formatting | bytes 196608 | tf_op jit(solution)/shard_map/reshape | solution.py:126
  11.0 0.7 reshape.204
  12.4 0.7 convert_select_fusion
  13.1 36.5 %all-reduce = (bf16[1,32,256]{2,1,0:T(8,128)(2,1)S(1)}, bf16[1,32,256]{2,1,0:T(8,128)(2,1)S(1)}) all-reduce(f32[1,32,256]{2,1,0:T(8,128)S(1)} %get-tuple-element.51, f32[1,32,256]{2,1,0:T(8,128)S(1)} %get-tuple-element.50), channel_id=1, replica_groups=mesh['groups'=2,'blk'=8,'mp'=2] {'blk'}, use_global_device_ids=true, to_apply=%region_1.2 | all-reduce | flops 16384 | bytes 98304 | tf_op jit(solution)/shard_map/psum | solution.py:75
  49.6 0.6 reshape.199
  50.2 30.5 %all_gather.6 = bf16[1,8,32,256]{3,2,0,1:T(8,128)(2,1)S(1)} all-gather(bf16[1,1,32,256]{3,2,0,1:T(8,128)(2,1)S(1)} %bitcast.86), channel_id=1, replica_groups=mesh['groups'=2,'blk'=8,'mp'=2] {'blk'}, dimensions={1}, use_global_device_ids=true | all-gather | bytes 147456 | tf_op jit(solution)/shard_map/all_gather | solution.py:101
  80.7 0.7 reshape.196
  81.4 30.5 %all_gather.7 = bf16[1,8,32,256]{3,2,0,1:T(8,128)(2,1)S(1)} all-gather(bf16[1,1,32,256]{3,2,0,1:T(8,128)(2,1)S(1)} %bitcast.87), channel_id=1, replica_groups=mesh['groups'=2,'blk'=8,'mp'=2] {'blk'}, dimensions={1}, use_global_device_ids=true | all-gather | bytes 147456 | tf_op jit(solution)/shard_map/all_gather | solution.py:102
  111.9 0.7 reshape.197
  112.6 0.8 reshape.194
  113.4 0.7 copy.42
  114.1 1.1 fusion.49
  115.2 0.6 copy-done.7
  115.8 0.7 reduce_max.41
  116.5 1.6 %fusion.50 = (f32[2,1344]{1,0:T(2,128)S(1)}, f32[2,1344,256]{2,1,0:T(8,128)S(1)}) fusion(bf16[256,2,128]{2,1,0:T(2,128)(2,1)} %reshape.196, bf16[2,1344,128]{2,0,1:T(2,128)(2,1)S(1)} %bitcast.79), kind=kOutput, calls=%fused_computation.76 | convolution fusion | flops 177534336 | bytes 3582464 | tf_op jit(solution)/shard_map/while/body/eval_jaxpr/grd,gnd->grn/dot_general | solution.py:96
  118.1 0.6 fusion.48
  118.7 0.7 max.104
  119.4 1.4 %fusion.1 = f32[2,1344]{1,0:T(2,128)} fusion(f32[2,1344,256]{2,1,0:T(8,128)S(1)} %get-tuple-element.45, f32[2,1344]{1,0:T(2,128)S(1)} %get-tuple-element.41), kind=kLoop, calls=%fused_computation.5 | loop fusion | flops 1373568 | bytes 2774016 | tf_op jit(solution)/shard_map/while/body/eval_jaxpr/reduce_sum | solution.py:27
  120.8 1.9 %fusion.52 = (f32[2,6,224]{2,1,0:T(8,128)}, f32[2,6,224,32]{2,3,1,0:T(8,128)}) fusion(bf16[2,6,224,128]{3,0,2,1:T(2,128)(2,1)S(1)} %bitcast.80, bf16[6,32,2,128]{3,2,1,0:T(2,128)(2,1)S(1)} %copy-done.4), kind=kOutput, calls=%fused_computation.78 | convolution fusion | flops 22189440 | bytes 1141248 | tf_op jit(solution)/shard_map/gsrd,gsnd->gsrn/dot_general | solution.py:128
  122.7 1.3 fusion
  124.1 0.4 convolution_add_fusion
  124.5 0.1 fusion.19
  124.6 0.1 reduce_sum.44
  124.7 0.1 copy-done.13
  124.8 0.1 reduce_sum.42
  124.8 0.0 collective-permute-done.1
  124.8 0.7 slice.30
  125.6 0.9 slice.31
  126.5 0.7 slice.27
  127.2 0.9 slice.28
  128.2 0.5 fusion.51
  128.8 0.1 fusion.15
  128.9 0.2 copy-done.1
  129.1 0.1 fusion.17
  129.2 1.3 fusion.4
  130.5 0.7 fusion.5
  131.2 0.7 copy.60
  131.9 0.1 copy.61
  132.0 0.7 reshape.207
  132.8 1.0 fusion.10
  (42 shorter events, 0.2 us)
Async XLA Ops:
  0.0 50.2 %copy-start.16 = (bf16[1,1,32,256]{3,2,1,0:T(8,128)(2,1)S(1)}, bf16[1,1,32,256]{3,2,1,0:T(8,128)(2,1)}, u32[]{:S(2)}) copy-start(bf16[1,1,32,256]{3,2,1,0:T(8,128)(2,1)} %param.21) | copy-start | bytes 49156
  0.0 81.4 %copy-start.17 = (bf16[1,1,32,256]{3,2,1,0:T(8,128)(2,1)S(1)}, bf16[1,1,32,256]{3,2,1,0:T(8,128)(2,1)}, u32[]{:S(2)}) copy-start(bf16[1,1,32,256]{3,2,1,0:T(8,128)(2,1)} %param.22) | copy-start | bytes 49156
  0.0 112.6 %copy-start.2 = (bf16[6,1,32,1792]{3,2,1,0:T(8,128)(2,1)S(1)}, bf16[6,1,32,1792]{3,2,1,0:T(8,128)(2,1)}, u32[]{:S(2)}) copy-start(bf16[6,1,32,1792]{3,2,1,0:T(8,128)(2,1)} %param.13) | copy-start | bytes 2064388
  5.0 119.9 %collective-permute-start.1 = (bf16[6,1,32,256]{3,2,1,0:T(8,128)(2,1)}, bf16[6,1,32,256]{3,2,1,0:T(8,128)(2,1)}, u32[]{:S(2)}, u32[]{:S(2)}) collective-permute-start(bf16[6,1,32,256]{3,2,1,0:T(8,128)(2,1)} %get-tuple-element.36), channel_id=1, source_target_pairs={{14,0},{0,2},{2,4},{4,6},{6,8},{8,10},{10,12},{12,14},{15,1},{1,3}... | collective-permute-start | bytes 294920 | tf_op jit(solution)/shard_map/ppermute | solution.py:15
  7.9 118.5 %collective-permute-start = (bf16[6,1,32,256]{3,2,1,0:T(8,128)(2,1)S(1)}, bf16[6,1,32,256]{3,2,1,0:T(8,128)(2,1)}, u32[]{:S(2)}, u32[]{:S(2)}) collective-permute-start(bf16[6,1,32,256]{3,2,1,0:T(8,128)(2,1)S(1)} %get-tuple-element.37), channel_id=1, source_target_pairs={{14,0},{0,2},{2,4},{4,6},{6,8},{8,10},{10,12},{12,14},{15,1},{1,3}... | collective-permute-start | bytes 294920 | tf_op jit(solution)/shard_map/ppermute | solution.py:15
  115.2 0.6 copy-start.7
  116.5 1.6 %copy-start.8 = (f32[2,1344]{1,0:T(2,128)S(1)}, f32[2,1344]{1,0:T(2,128)}, u32[]{:S(2)}) copy-start(f32[2,1344]{1,0:T(2,128)} %copy-done.7) | copy-start | bytes 32260
  119.4 1.5 %copy-start.4 = (bf16[6,32,2,128]{3,2,1,0:T(2,128)(2,1)S(1)}, bf16[6,32,2,128]{3,2,1,0:T(2,128)(2,1)}, u32[]{:S(2)}) copy-start(bf16[6,32,2,128]{3,2,1,0:T(2,128)(2,1)} %reshape.204) | copy-start | bytes 294916
  119.4 3.3 %copy-start.3 = (bf16[256,2,128]{2,1,0:T(2,128)(2,1)S(1)}, bf16[256,2,128]{2,1,0:T(2,128)(2,1)}, u32[]{:S(2)}) copy-start(bf16[256,2,128]{2,1,0:T(2,128)(2,1)} %reshape.197) | copy-start | bytes 393220
  119.4 3.3 %copy-start.14 = (f32[2,1344]{1,0:T(2,128)S(1)}, f32[2,1344]{1,0:T(2,128)}, u32[]{:S(2)}) copy-start(f32[2,1344]{1,0:T(2,128)} %get-tuple-element.39) | copy-start | bytes 32260
  119.4 3.3 %copy-start.15 = (f32[2,1344]{1,0:T(2,128)S(1)}, f32[2,1344]{1,0:T(2,128)}, u32[]{:S(2)}) copy-start(f32[2,1344]{1,0:T(2,128)} %get-tuple-element.40) | copy-start | bytes 32260
  122.7 1.3 copy-start
  122.7 1.3 copy-start.6
  122.7 1.3 copy-start.10
  124.0 0.7 copy-start.13
  124.5 4.2 %copy-start.5 = (f32[2,6,224]{2,1,0:T(8,128)S(1)}, f32[2,6,224]{2,1,0:T(8,128)}, u32[]{:S(2)}) copy-start(f32[2,6,224]{2,1,0:T(8,128)} %max.104) | copy-start | bytes 32260
  124.6 4.2 %copy-start.12 = (f32[2,6,224]{2,1,0:T(8,128)S(1)}, f32[2,6,224]{2,1,0:T(8,128)}, u32[]{:S(2)}) copy-start(f32[2,6,224]{2,1,0:T(8,128)} %reduce_max.41) | copy-start | bytes 32260
  128.1 0.8 copy-start.11
  128.1 1.0 copy-start.1
  129.2 1.3 copy-start.9
where the time goes:
time: 135 us; the launch traced here: 134 us
  blocking collectives  97.5 us (72%)
  local copies, waits for them, and re-layouts  13.2 us (10%)
  matrix products  9.66 us (7%)
  other arithmetic  8.06 us (6%)
  starting transfers between devices  4.49 us (3%)
    psum x1, blocking collectives, on_device(): lax.psum((jnp.where(mine, completed_keys.astype(jnp.float32), 0.0), jnp.w...  36.5 us
    all_gather x1, blocking collectives, on_device(): lax.all_gather(prefix_key_cache, 'blk', axis=1, tiled=True)  30.5 us
    all_gather x1, blocking collectives, on_device(): lax.all_gather(prefix_value_cache, 'blk', axis=1, tiled=True)  30.5 us
    ppermute x2, starting transfers between devices, shifted(): return lax.ppermute(block, axis, route)  4.49 us
    dot_general x4, matrix products, absorb(): jnp.einsum(form, weight.astype(jnp.bfloat16), values, preferred_element_t...  3.6 us
  transfers between devices with their start and end apart: 2, of which 0 were waited for; matrix products, arithmetic and copies ran while one was open for 13% of the time, Pallas kernels for 0%

commit v1 on v0

v1 whole, which is shorter than its diff:
```python
import functools
import math

import jax
import jax.numpy as jnp
from jax import lax
from jax.experimental import pallas as pl
from jax.experimental.pallas import tpu as pltpu
from jax.sharding import PartitionSpec as P

QUERY_GROUPS = 28
MEMORY_GROUPS = 4
FEATURE_DIM = 128
UNMASK = 4
GROUP = QUERY_GROUPS // MEMORY_GROUPS
CHUNK = 8
MESH = pl.DeviceIdType.MESH
F32 = jnp.float32
BF16 = jnp.bfloat16


def over_rows(a, b):
    return lax.dot_general(a, b, (((0,), (0,)), ((), ())), preferred_element_type=F32)


def over_lanes(a, b):
    return lax.dot_general(a, b, (((1,), (1,)), ((), ())), preferred_element_type=F32)


def kernel(
    n,
    order_hbm,
    rounds_hbm,
    choice_hbm,
    index_hbm,
    noise_k_hbm,
    noise_v_hbm,
    q_hbm,
    uk_hbm,
    uv_hbm,
    pk_hbm,
    pv_hbm,
    ck_hbm,
    cv_hbm,
    out_hbm,
    order_ref,
    rounds_ref,
    choice_ref,
    index_ref,
    table,
    q,
    uk,
    uv,
    own,
    prev,
    gath,
    maskf,
    res,
    local_sem,
    out_sem,
    gsend,
    grecv,
    ssend,
    srecv,
):
    slots, block, _ = own.shape
    width = noise_k_hbm.shape[1]
    heads = width // FEATURE_DIM
    me = lax.axis_index("blk")
    barrier = pltpu.get_barrier_semaphore()

    @pl.loop(1, n)
    def _(d):
        pl.semaphore_signal(
            barrier, inc=1, device_id={"blk": lax.rem(me + d, n)}, device_id_type=MESH
        )

    loads = [
        pltpu.make_async_copy(src, dst, local_sem.at[i])
        for i, (src, dst) in enumerate(
            (
                (order_hbm, order_ref),
                (rounds_hbm, rounds_ref),
                (choice_hbm, choice_ref),
                (noise_k_hbm, table.at[:, pl.ds(0, width)]),
                (noise_v_hbm, table.at[:, pl.ds(width, width)]),
                (uk_hbm.at[:, 0], uk),
                (uv_hbm.at[:, 0], uv),
                (pk_hbm.at[0, 0], gath.at[me, pl.ds(0, block), pl.ds(0, width)]),
                (pv_hbm.at[0, 0], gath.at[me, pl.ds(0, block), pl.ds(width, width)]),
                (ck_hbm.at[0], gath.at[me, pl.ds(block, block), pl.ds(0, width)]),
                (cv_hbm.at[0], gath.at[me, pl.ds(block, block), pl.ds(width, width)]),
                (index_hbm, index_ref),
                (q_hbm.at[:, 0], q),
            )
        )
    ]
    for load in loads:
        load.start()
    for load in loads[:7]:
        load.wait()

    entries = table.shape[0]
    row_n = lax.broadcasted_iota(jnp.int32, (entries, block), 0)
    row_b = lax.broadcasted_iota(jnp.int32, (block, block), 0)
    col_b = lax.broadcasted_iota(jnp.int32, (block, block), 1)
    ones_n = jnp.ones((entries, FEATURE_DIM), BF16)
    for s in range(slots):
        hidden = order_ref[s] >= UNMASK * rounds_ref[s]
        noise = jnp.where((row_n == choice_ref[s]) & hidden, 1.0, 0.0).astype(BF16)
        keep = jnp.where((row_b == col_b) & jnp.logical_not(hidden), 1.0, 0.0).astype(BF16)
        shown = jnp.concatenate([uk[s], uv[s]], axis=1)
        own[s] = over_rows(
            jnp.concatenate([noise, keep], axis=0), jnp.concatenate([table[...], shown], axis=0)
        ).astype(BF16)
        maskf[s] = over_rows(noise, ones_n)

    for load in loads[7:11]:
        load.wait()
    pl.semaphore_wait(barrier, n - 1)

    after = lax.rem(me + 1, n)
    wrap = me // (n - 1)

    def shift(s):
        to = lax.rem(s + wrap, slots)
        return pltpu.make_async_remote_copy(
            src_ref=own.at[s],
            dst_ref=prev.at[to],
            send_sem=ssend.at[s],
            recv_sem=srecv.at[to],
            device_id={"blk": after},
            device_id_type=MESH,
        )

    def spread(d):
        return pltpu.make_async_remote_copy(
            src_ref=gath.at[me],
            dst_ref=gath.at[me],
            send_sem=gsend.at[d],
            recv_sem=grecv.at[me],
            device_id={"blk": lax.rem(me + d, n)},
            device_id_type=MESH,
        )

    def spread_in(d):
        j = lax.rem(me + d, n)
        return pltpu.make_async_remote_copy(
            src_ref=gath.at[j],
            dst_ref=gath.at[j],
            send_sem=gsend.at[d],
            recv_sem=grecv.at[j],
            device_id={"blk": j},
            device_id_type=MESH,
        )

    def shift_in(s):
        return pltpu.make_async_remote_copy(
            src_ref=own.at[s],
            dst_ref=prev.at[s],
            send_sem=ssend.at[s],
            recv_sem=srecv.at[s],
            device_id={"blk": after},
            device_id_type=MESH,
        )

    @pl.loop(1, n)
    def _(d):
        spread(d).start()

    for s in range(slots):
        shift(s).start()

    loads[11].wait()
    loads[12].wait()

    @pl.loop(1, n)
    def _(d):
        spread_in(d).wait_recv()

    factor = FEATURE_DIM**-0.5 * math.log2(math.e)
    owner = index_ref[0]
    commit = gath[owner, block:, :]

    def lanes(g):
        return slice(g * FEATURE_DIM, (g + 1) * FEATURE_DIM)

    def with_ones(v):
        return jnp.concatenate([v, jnp.ones(v.shape, BF16)], axis=1)

    def shared(c, col):
        part = gath[pl.ds(c * CHUNK, CHUNK), 0:block, col]
        return part.reshape(CHUNK * block, FEATURE_DIM)

    @pl.loop(0, slots)
    def _(s):
        shift_in(s).wait_recv()
        for g in range(heads):
            first = g * GROUP
            qs = jnp.concatenate([q[s, :, lanes(first + r)] for r in range(GROUP)], axis=0)
            kc, vc = lanes(g), lanes(heads + g)
            k2 = jnp.concatenate([prev[s, :, kc], own[s, :, kc], commit[:, kc]], axis=0)
            v2 = jnp.concatenate([prev[s, :, vc], own[s, :, vc], commit[:, vc]], axis=0)
            s1 = over_lanes(qs, shared(0, kc))
            s2 = over_lanes(qs, k2)
            top = jnp.maximum(
                jnp.max(s1, axis=1, keepdims=True), jnp.max(s2, axis=1, keepdims=True)
            )
            p1 = jnp.exp2((s1 - top) * factor).astype(BF16)
            p2 = jnp.exp2((s2 - top) * factor).astype(BF16)
            acc = jnp.dot(p1, with_ones(shared(0, vc)), preferred_element_type=F32)
            acc = acc + jnp.dot(p2, with_ones(v2), preferred_element_type=F32)
            if n > CHUNK:

                def more(c, state):
                    top, acc = state
                    s1 = over_lanes(qs, shared(c, kc))
                    new = jnp.maximum(top, jnp.max(s1, axis=1, keepdims=True))
                    p1 = jnp.exp2((s1 - new) * factor).astype(BF16)
                    part = jnp.dot(p1, with_ones(shared(c, vc)), preferred_element_type=F32)
                    return new, acc * jnp.exp2((top - new) * factor) + part

                top, acc = lax.fori_loop(1, n // CHUNK, more, (top, acc))
            o = acc[:, :FEATURE_DIM] / acc[:, FEATURE_DIM:]
            mask = maskf[s]
            for r in range(GROUP):
                part = o[r * block : (r + 1) * block] * mask
                res[s, :, lanes(first + r)] = part.astype(BF16)
        pltpu.make_async_copy(res.at[s], out_hbm.at[s, 0], out_sem.at[s]).start()

    @pl.loop(1, n)
    def _(d):
        spread(d).wait_send()

    for s in range(slots):
        shift_in(s).wait_send()
        pltpu.make_async_copy(res.at[s], out_hbm.at[s, 0], out_sem.at[s]).wait()


def on_device(
    n,
    probe_vectors,
    unsettled_lookups,
    unsettled_payloads,
    uncover_ordering,
    rounds_finished,
    random_entry_choice,
    noise_token_keys,
    noise_token_values,
    prefix_key_cache,
    prefix_value_cache,
    completed_keys,
    completed_values,
    committing_index,
):
    slots, _, block, columns = probe_vectors.shape
    width = noise_token_keys.shape[1]
    anywhere = pl.BlockSpec(memory_space=pl.ANY)
    return pl.pallas_call(
        functools.partial(kernel, n),
        out_shape=jax.ShapeDtypeStruct(probe_vectors.shape, BF16),
        in_specs=[pl.BlockSpec(memory_space=pltpu.HBM)] * 13,
        out_specs=anywhere,
        scratch_shapes=[
            pltpu.VMEM(uncover_ordering.shape, jnp.int32),
            pltpu.SMEM((slots,), jnp.int32),
            pltpu.VMEM(random_entry_choice.shape, jnp.int32),
            pltpu.SMEM((1,), jnp.int32),
            pltpu.VMEM((noise_token_keys.shape[0], 2 * width), BF16),
            pltpu.VMEM((slots, block, columns), BF16),
            pltpu.VMEM((slots, block, width), BF16),
            pltpu.VMEM((slots, block, width), BF16),
            pltpu.VMEM((slots, block, 2 * width), BF16),
            pltpu.VMEM((slots, block, 2 * width), BF16),
            pltpu.VMEM((n, 2 * block, 2 * width), BF16),
            pltpu.VMEM((slots, block, FEATURE_DIM), F32),
            pltpu.VMEM((slots, block, columns), BF16),
            pltpu.SemaphoreType.DMA((13,)),
            pltpu.SemaphoreType.DMA((slots,)),
            pltpu.SemaphoreType.DMA((n,)),
            pltpu.SemaphoreType.DMA((n,)),
            pltpu.SemaphoreType.DMA((slots,)),
            pltpu.SemaphoreType.DMA((slots,)),
        ],
        compiler_params=pltpu.CompilerParams(
            collective_id=0, has_side_effects=True, vmem_limit_bytes=60 * 2**20
        ),
    )(
        uncover_ordering,
        rounds_finished.reshape(slots),
        random_entry_choice,
        committing_index,
        noise_token_keys,
        noise_token_values,
        probe_vectors,
        unsettled_lookups,
        unsettled_payloads,
        prefix_key_cache,
        prefix_value_cache,
        completed_keys,
        completed_values,
    )


def solution(mesh):
    wide = P("groups", "blk", None, "mp")
    placed = (
        wide,
        wide,
        wide,
        P("groups", "blk", None),
        P("groups", "blk"),
        P("groups", "blk", None),
        P(None, "mp"),
        P(None, "mp"),
        wide,
        wide,
        P(("groups", "blk"), None, "mp"),
        P(("groups", "blk"), None, "mp"),
        P("groups"),
    )
    return jax.shard_map(
        functools.partial(on_device, mesh.shape["blk"]),
        mesh=mesh,
        in_specs=placed,
        out_specs=wide,
        check_vma=False,
    )
```

time: 135 us -> 29.9 us (0.22)
  blocking collectives: 97.5 us -> 0 us
  Pallas kernels: 0 us -> 27.1 us
  local copies, waits for them, and re-layouts: 13.2 us -> 1.99 us
  matrix products: 9.66 us -> 0 us
  other arithmetic: 8.06 us -> 0 us
  starting transfers between devices: 4.49 us -> 0 us
    all_gather x2 -> x0, blocking collectives: 61 us -> none  [the longest x1 30.5 us: on_device(): lax.all_gather(prefix_key_cache, 'blk', axis=1, tiled=True)]
    psum x1 -> x0, blocking collectives: 36.5 us -> none  [on_device(): lax.psum((jnp.where(mine, completed_keys.astype(jnp.float32), 0.0), jnp.w...]
    pallas_call x0 -> x1, Pallas kernels: none -> 27.1 us  [on_device(): pl.pallas_call(functools.partial(kernel, n), out_shape=jax.ShapeDtypeStru...]
    dot_general x9 -> x0, matrix products: 9.66 us -> none  [the longest x4 3.6 us: absorb(): jnp.einsum(form, weight.astype(jnp.bfloat16), values, preferred_element_t...]
    reshape x10 -> x0, local copies, waits for them, and re-layouts: 5.81 us -> none  [the longest x4 2 us: arrange(): return jnp.transpose(tensor.reshape(-1, heads, FEATURE_DIM), (1, 0, 2))]
    ppermute x2 -> x0, starting transfers between devices: 4.49 us -> none  [shifted(): return lax.ppermute(block, axis, route)]
    slice x4 -> x0, local copies, waits for them, and re-layouts: 3.22 us -> none  [the longest x2 1.61 us: on_device(): prev_keys = jnp.where(first, jnp.roll(got_keys, 1, axis=0), got_keys)]
    select_n x3 -> x0, other arithmetic: 2.46 us -> none  [the longest x1 1.67 us: on_device(): jnp.where(concealed_flags[..., None], still_noised[..., reveal_width:], u...]
  transfers between devices with their start and end apart: 2 -> 0, of which waited for: 0 -> 0; matrix products, arithmetic and copies ran while one was open for 13% -> 0% of each run, Pallas kernels for 0% -> 0%
where the time goes in v1:
time: 29.9 us; the launch traced here: 29.7 us
  Pallas kernels  27.1 us (91%)
  local copies, waits for them, and re-layouts  1.99 us (7%)
  between operations  0.66 us (2%)
    pallas_call x1, Pallas kernels, on_device(): pl.pallas_call(functools.partial(kernel, n), out_shape=jax.ShapeDtypeStru...  27.1 us
    unnamed x1, local copies, waits for them, and re-layouts  1.99 us

profile of v1, /device:TPU:0, one launch (start us, length us, event | category | flops | bytes accessed | tf_op | source)
XLA Modules:
  0.0 29.7 jit_solution(13415842973396335737)
XLA Ops:
  0.7 27.1 %shard_map.127 = bf16[6,1,32,1792]{3,2,1,0:T(8,128)(2,1)} custom-call(s32[6,1,32]{2,1,0:T(1,128)} %order_hbm.1, s32[6]{0:T(128)} %bitcast.1, s32[6,1,32]{2,1,0:T(1,128)} %choice_hbm.1, s32[1]{0:T(128)S(6)} %copy.15.index_hbm, bf16[64,256]{1,0:T(8,128)(2,1)} %noise_k_hbm.1, bf16[64,256]{1,0:T(8,128)(2,1)} %noise_v_hbm.1, bf16[6,1,32,1792]{3,2,1,0:T(8,128)(2,1)} %q_hbm.1, ...), custom_call_target="tpu_custom_call" | custom-call | tf_op jit(solution)/shard_map/pallas_call | solution.py:259
  27.7 2.0 %copy.16 = bf16[6,1,32,1792]{3,2,1,0:T(8,128)(2,1)} copy(bf16[6,1,32,1792]{3,2,1,0:T(8,128)(2,1)} %shard_map.127) | data formatting | bytes 1376256

commit v2 on v1

--- a/solution.py
+++ b/solution.py
@@ -13,7 +13,7 @@
 FEATURE_DIM = 128
 UNMASK = 4
 GROUP = QUERY_GROUPS // MEMORY_GROUPS
-CHUNK = 8
+HALF = 4
 MESH = pl.DeviceIdType.MESH
 F32 = jnp.float32
 BF16 = jnp.bfloat16
@@ -42,7 +42,7 @@
     pv_hbm,
     ck_hbm,
     cv_hbm,
-    out_hbm,
+    out,
     order_ref,
     rounds_ref,
     choice_ref,
@@ -53,13 +53,15 @@
     uv,
     own,
     prev,
-    gath,
+    col,
+    oth,
+    com,
     maskf,
-    res,
     local_sem,
-    out_sem,
     gsend,
     grecv,
+    fsend,
+    frecv,
     ssend,
     srecv,
 ):
@@ -69,11 +71,18 @@
     me = lax.axis_index("blk")
     barrier = pltpu.get_barrier_semaphore()
 
-    @pl.loop(1, n)
-    def _(d):
+    rows = n // 2
+    row, par = me // 2, lax.rem(me, 2)
+    partner = me + 1 - 2 * par
+
+    def greet(d):
         pl.semaphore_signal(
             barrier, inc=1, device_id={"blk": lax.rem(me + d, n)}, device_id_type=MESH
         )
+
+    greet(1)
+    greet(n - 1)
+    pl.loop(1, rows)(lambda d: greet(2 * d))
 
     loads = [
         pltpu.make_async_copy(src, dst, local_sem.at[i])
@@ -86,10 +95,10 @@
                 (noise_v_hbm, table.at[:, pl.ds(width, width)]),
                 (uk_hbm.at[:, 0], uk),
                 (uv_hbm.at[:, 0], uv),
-                (pk_hbm.at[0, 0], gath.at[me, pl.ds(0, block), pl.ds(0, width)]),
-                (pv_hbm.at[0, 0], gath.at[me, pl.ds(0, block), pl.ds(width, width)]),
-                (ck_hbm.at[0], gath.at[me, pl.ds(block, block), pl.ds(0, width)]),
-                (cv_hbm.at[0], gath.at[me, pl.ds(block, block), pl.ds(width, width)]),
+                (pk_hbm.at[0, 0], col.at[row, pl.ds(0, block), pl.ds(0, width)]),
+                (pv_hbm.at[0, 0], col.at[row, pl.ds(0, block), pl.ds(width, width)]),
+                (ck_hbm.at[0], col.at[row, pl.ds(block, block), pl.ds(0, width)]),
+                (cv_hbm.at[0], col.at[row, pl.ds(block, block), pl.ds(width, width)]),
                 (index_hbm, index_ref),
                 (q_hbm.at[:, 0], q),
             )
@@ -117,7 +126,7 @@
 
     for load in loads[7:11]:
         load.wait()
-    pl.semaphore_wait(barrier, n - 1)
+    pl.semaphore_wait(barrier, rows + 1)
 
     after = lax.rem(me + 1, n)
     wrap = me // (n - 1)
@@ -135,22 +144,41 @@
 
     def spread(d):
         return pltpu.make_async_remote_copy(
-            src_ref=gath.at[me],
-            dst_ref=gath.at[me],
+            src_ref=col.at[row],
+            dst_ref=col.at[row],
             send_sem=gsend.at[d],
-            recv_sem=grecv.at[me],
-            device_id={"blk": lax.rem(me + d, n)},
-            device_id_type=MESH,
-        )
-
-    def spread_in(d):
-        j = lax.rem(me + d, n)
-        return pltpu.make_async_remote_copy(
-            src_ref=gath.at[j],
-            dst_ref=gath.at[j],
-            send_sem=gsend.at[d],
+            recv_sem=grecv.at[row],
+            device_id={"blk": 2 * lax.rem(row + d, rows) + par},
+            device_id_type=MESH,
+        )
+
+    def spread_in(j):
+        return pltpu.make_async_remote_copy(
+            src_ref=col.at[j],
+            dst_ref=col.at[j],
+            send_sem=gsend.at[0],
             recv_sem=grecv.at[j],
-            device_id={"blk": j},
+            device_id={"blk": partner},
+            device_id_type=MESH,
+        )
+
+    def relay(j):
+        return pltpu.make_async_remote_copy(
+            src_ref=col.at[j, pl.ds(0, block)],
+            dst_ref=oth.at[j],
+            send_sem=fsend.at[j],
+            recv_sem=frecv.at[j],
+            device_id={"blk": partner},
+            device_id_type=MESH,
+        )
+
+    def chosen(mine):
+        return pltpu.make_async_remote_copy(
+            src_ref=com.at[mine],
+            dst_ref=com.at[mine],
+            send_sem=fsend.at[rows],
+            recv_sem=frecv.at[rows],
+            device_id={"blk": partner},
             device_id_type=MESH,
         )
 
@@ -164,23 +192,36 @@
             device_id_type=MESH,
         )
 
-    @pl.loop(1, n)
+    @pl.loop(1, rows)
     def _(d):
         spread(d).start()
 
+    relay(row).start()
+
     for s in range(slots):
         shift(s).start()
 
     loads[11].wait()
+    owner = index_ref[0]
+
+    @pl.loop(1, rows)
+    def _(d):
+        j = lax.rem(row + d, rows)
+        spread_in(j).wait_recv()
+        relay(j).start()
+
+    com[par] = col[owner // 2, block:, :]
+    chosen(par).start()
     loads[12].wait()
 
-    @pl.loop(1, n)
-    def _(d):
-        spread_in(d).wait_recv()
+    @pl.loop(0, rows)
+    def _(j):
+        relay(j).wait_recv()
+
+    chosen(1 - par).wait_recv()
 
     factor = FEATURE_DIM**-0.5 * math.log2(math.e)
-    owner = index_ref[0]
-    commit = gath[owner, block:, :]
+    commit = com[lax.rem(owner, 2)]
 
     def lanes(g):
         return slice(g * FEATURE_DIM, (g + 1) * FEATURE_DIM)
@@ -188,11 +229,12 @@
     def with_ones(v):
         return jnp.concatenate([v, jnp.ones(v.shape, BF16)], axis=1)
 
-    def shared(c, col):
-        part = gath[pl.ds(c * CHUNK, CHUNK), 0:block, col]
-        return part.reshape(CHUNK * block, FEATURE_DIM)
-
-    @pl.loop(0, slots)
+    def shared(c, where):
+        near = col[pl.ds(c * HALF, HALF), 0:block, where].reshape(HALF * block, FEATURE_DIM)
+        far = oth[pl.ds(c * HALF, HALF), :, where].reshape(HALF * block, FEATURE_DIM)
+        return jnp.concatenate([near, far], axis=0)
+
+    @pl.loop(0, slots, unroll=2)
     def _(s):
         shift_in(s).wait_recv()
         for g in range(heads):
@@ -210,7 +252,7 @@
             p2 = jnp.exp2((s2 - top) * factor).astype(BF16)
             acc = jnp.dot(p1, with_ones(shared(0, vc)), preferred_element_type=F32)
             acc = acc + jnp.dot(p2, with_ones(v2), preferred_element_type=F32)
-            if n > CHUNK:
+            if rows > HALF:
 
                 def more(c, state):
                     top, acc = state
@@ -220,21 +262,25 @@
                     part = jnp.dot(p1, with_ones(shared(c, vc)), preferred_element_type=F32)
                     return new, acc * jnp.exp2((top - new) * factor) + part
 
-                top, acc = lax.fori_loop(1, n // CHUNK, more, (top, acc))
+                top, acc = lax.fori_loop(1, rows // HALF, more, (top, acc))
             o = acc[:, :FEATURE_DIM] / acc[:, FEATURE_DIM:]
             mask = maskf[s]
             for r in range(GROUP):
                 part = o[r * block : (r + 1) * block] * mask
-                res[s, :, lanes(first + r)] = part.astype(BF16)
-        pltpu.make_async_copy(res.at[s], out_hbm.at[s, 0], out_sem.at[s]).start()
-
-    @pl.loop(1, n)
+                out[s, 0, :, lanes(first + r)] = part.astype(BF16)
+
+    @pl.loop(1, rows)
     def _(d):
         spread(d).wait_send()
 
+    @pl.loop(0, rows)
+    def _(j):
+        relay(j).wait_send()
+
+    chosen(par).wait_send()
+
     for s in range(slots):
         shift_in(s).wait_send()
-        pltpu.make_async_copy(res.at[s], out_hbm.at[s, 0], out_sem.at[s]).wait()
 
 
 def on_device(
@@ -258,9 +304,9 @@
     anywhere = pl.BlockSpec(memory_space=pl.ANY)
     return pl.pallas_call(
         functools.partial(kernel, n),
-        out_shape=jax.ShapeDtypeStruct(probe_vectors.shape, BF16),
+        out_shape=pltpu.VMEM(probe_vectors.shape, BF16),
         in_specs=[pl.BlockSpec(memory_space=pltpu.HBM)] * 13,
-        out_specs=anywhere,
+        out_specs=pl.BlockSpec(memory_space=pltpu.VMEM),
         scratch_shapes=[
             pltpu.VMEM(uncover_ordering.shape, jnp.int32),
             pltpu.SMEM((slots,), jnp.int32),
@@ -272,13 +318,15 @@
             pltpu.VMEM((slots, block, width), BF16),
             pltpu.VMEM((slots, block, 2 * width), BF16),
             pltpu.VMEM((slots, block, 2 * width), BF16),
-            pltpu.VMEM((n, 2 * block, 2 * width), BF16),
+            pltpu.VMEM((n // 2, 2 * block, 2 * width), BF16),
+            pltpu.VMEM((n // 2, block, 2 * width), BF16),
+            pltpu.VMEM((2, block, 2 * width), BF16),
             pltpu.VMEM((slots, block, FEATURE_DIM), F32),
-            pltpu.VMEM((slots, block, columns), BF16),
             pltpu.SemaphoreType.DMA((13,)),
-            pltpu.SemaphoreType.DMA((slots,)),
-            pltpu.SemaphoreType.DMA((n,)),
-            pltpu.SemaphoreType.DMA((n,)),
+            pltpu.SemaphoreType.DMA((n // 2,)),
+            pltpu.SemaphoreType.DMA((n // 2,)),
+            pltpu.SemaphoreType.DMA((n // 2 + 1,)),
+            pltpu.SemaphoreType.DMA((n // 2 + 1,)),
             pltpu.SemaphoreType.DMA((slots,)),
             pltpu.SemaphoreType.DMA((slots,)),
         ],

time: 29.9 us -> 24 us (0.80)
  Pallas kernels: 27.1 us -> 22.3 us
  local copies, waits for them, and re-layouts: 1.99 us -> 0.85 us
    pallas_call x1, Pallas kernels: 27.1 us -> 22.3 us  [on_device(): pl.pallas_call(functools.partial(kernel, n), out_shape=pltpu.VMEM(probe_v...]
    unnamed x1, local copies, waits for them, and re-layouts: 1.99 us -> 0.85 us
where the time goes in v2:
time: 24 us; the launch traced here: 23.8 us
  Pallas kernels  22.3 us (93%)
  local copies, waits for them, and re-layouts  0.85 us (4%)
  between operations  0.66 us (3%)
    pallas_call x1, Pallas kernels, on_device(): pl.pallas_call(functools.partial(kernel, n), out_shape=pltpu.VMEM(probe_v...  22.3 us
    unnamed x1, local copies, waits for them, and re-layouts  0.85 us

profile of v2, /device:TPU:0, one launch (start us, length us, event | category | flops | bytes accessed | tf_op | source)
XLA Modules:
  0.0 23.8 jit_solution(11086664380511888418)
XLA Ops:
  0.7 22.3 %shard_map.127 = bf16[6,1,32,1792]{3,2,1,0:T(8,128)(2,1)S(1)} custom-call(s32[6,1,32]{2,1,0:T(1,128)} %order_hbm.1, s32[6]{0:T(128)} %bitcast.1, s32[6,1,32]{2,1,0:T(1,128)} %choice_hbm.1, s32[1]{0:T(128)S(6)} %copy.16.index_hbm, bf16[64,256]{1,0:T(8,128)(2,1)} %noise_k_hbm.1, bf16[64,256]{1,0:T(8,128)(2,1)} %noise_v_hbm.1, bf16[6,1,32,1792]{3,2,1,0:T(8,128)(2,1)} %q_hbm.1, ...), custom_call_target="tpu_custom_call" | custom-call | tf_op jit(solution)/shard_map/pallas_call | solution.py:305
  22.9 0.8 %copy.15 = bf16[6,1,32,1792]{3,2,1,0:T(8,128)(2,1)} copy(bf16[6,1,32,1792]{3,2,1,0:T(8,128)(2,1)S(1)} %shard_map.127) | data formatting | bytes 1376256

commit v3 on v2

--- a/solution.py
+++ b/solution.py
@@ -56,12 +56,17 @@
     col,
     oth,
     com,
+    cand,
+    pair,
+    half,
     maskf,
     local_sem,
     gsend,
     grecv,
     fsend,
     frecv,
+    hsend,
+    hrecv,
     ssend,
     srecv,
 ):
@@ -95,10 +100,10 @@
                 (noise_v_hbm, table.at[:, pl.ds(width, width)]),
                 (uk_hbm.at[:, 0], uk),
                 (uv_hbm.at[:, 0], uv),
-                (pk_hbm.at[0, 0], col.at[row, pl.ds(0, block), pl.ds(0, width)]),
-                (pv_hbm.at[0, 0], col.at[row, pl.ds(0, block), pl.ds(width, width)]),
-                (ck_hbm.at[0], col.at[row, pl.ds(block, block), pl.ds(0, width)]),
-                (cv_hbm.at[0], col.at[row, pl.ds(block, block), pl.ds(width, width)]),
+                (pk_hbm.at[0, 0], col.at[row, :, pl.ds(0, width)]),
+                (pv_hbm.at[0, 0], col.at[row, :, pl.ds(width, width)]),
+                (ck_hbm.at[0], cand.at[0]),
+                (cv_hbm.at[0], cand.at[1]),
                 (index_hbm, index_ref),
                 (q_hbm.at[:, 0], q),
             )
@@ -164,10 +169,40 @@
 
     def relay(j):
         return pltpu.make_async_remote_copy(
-            src_ref=col.at[j, pl.ds(0, block)],
+            src_ref=col.at[j],
             dst_ref=oth.at[j],
             send_sem=fsend.at[j],
             recv_sem=frecv.at[j],
+            device_id={"blk": partner},
+            device_id_type=MESH,
+        )
+
+    def swap(mine):
+        return pltpu.make_async_remote_copy(
+            src_ref=cand.at[1 - par],
+            dst_ref=pair.at[mine],
+            send_sem=hsend.at[0],
+            recv_sem=hrecv.at[rows],
+            device_id={"blk": partner},
+            device_id_type=MESH,
+        )
+
+    def pick(d):
+        return pltpu.make_async_remote_copy(
+            src_ref=half.at[row],
+            dst_ref=half.at[row],
+            send_sem=hsend.at[d],
+            recv_sem=hrecv.at[row],
+            device_id={"blk": 2 * lax.rem(row + d, rows) + par},
+            device_id_type=MESH,
+        )
+
+    def pick_in(j):
+        return pltpu.make_async_remote_copy(
+            src_ref=half.at[j],
+            dst_ref=half.at[j],
+            send_sem=hsend.at[0],
+            recv_sem=hrecv.at[j],
             device_id={"blk": partner},
             device_id_type=MESH,
         )
@@ -192,6 +227,8 @@
             device_id_type=MESH,
         )
 
+    swap(par).start()
+
     @pl.loop(1, rows)
     def _(d):
         spread(d).start()
@@ -203,6 +240,13 @@
 
     loads[11].wait()
     owner = index_ref[0]
+    pair[par] = cand[par]
+    swap(1 - par).wait_recv()
+    half[row] = pair[lax.rem(owner, 2)]
+
+    @pl.loop(1, rows)
+    def _(d):
+        pick(d).start()
 
     @pl.loop(1, rows)
     def _(d):
@@ -210,7 +254,11 @@
         spread_in(j).wait_recv()
         relay(j).start()
 
-    com[par] = col[owner // 2, block:, :]
+    @pl.loop(1, rows)
+    def _(d):
+        pick_in(lax.rem(row + d, rows)).wait_recv()
+
+    com[par] = half[owner // 2]
     chosen(par).start()
     loads[12].wait()
 
@@ -221,7 +269,6 @@
     chosen(1 - par).wait_recv()
 
     factor = FEATURE_DIM**-0.5 * math.log2(math.e)
-    commit = com[lax.rem(owner, 2)]
 
     def lanes(g):
         return slice(g * FEATURE_DIM, (g + 1) * FEATURE_DIM)
@@ -230,7 +277,7 @@
         return jnp.concatenate([v, jnp.ones(v.shape, BF16)], axis=1)
 
     def shared(c, where):
-        near = col[pl.ds(c * HALF, HALF), 0:block, where].reshape(HALF * block, FEATURE_DIM)
+        near = col[pl.ds(c * HALF, HALF), :, where].reshape(HALF * block, FEATURE_DIM)
         far = oth[pl.ds(c * HALF, HALF), :, where].reshape(HALF * block, FEATURE_DIM)
         return jnp.concatenate([near, far], axis=0)
 
@@ -241,8 +288,8 @@
             first = g * GROUP
             qs = jnp.concatenate([q[s, :, lanes(first + r)] for r in range(GROUP)], axis=0)
             kc, vc = lanes(g), lanes(heads + g)
-            k2 = jnp.concatenate([prev[s, :, kc], own[s, :, kc], commit[:, kc]], axis=0)
-            v2 = jnp.concatenate([prev[s, :, vc], own[s, :, vc], commit[:, vc]], axis=0)
+            k2 = jnp.concatenate([prev[s, :, kc], own[s, :, kc], com[0, :, lanes(g)]], axis=0)
+            v2 = jnp.concatenate([prev[s, :, vc], own[s, :, vc], com[1, :, lanes(g)]], axis=0)
             s1 = over_lanes(qs, shared(0, kc))
             s2 = over_lanes(qs, k2)
             top = jnp.maximum(
@@ -278,6 +325,11 @@
         relay(j).wait_send()
 
     chosen(par).wait_send()
+    swap(par).wait_send()
+
+    @pl.loop(1, rows)
+    def _(d):
+        pick(d).wait_send()
 
     for s in range(slots):
         shift_in(s).wait_send()
@@ -318,14 +370,19 @@
             pltpu.VMEM((slots, block, width), BF16),
             pltpu.VMEM((slots, block, 2 * width), BF16),
             pltpu.VMEM((slots, block, 2 * width), BF16),
-            pltpu.VMEM((n // 2, 2 * block, 2 * width), BF16),
             pltpu.VMEM((n // 2, block, 2 * width), BF16),
-            pltpu.VMEM((2, block, 2 * width), BF16),
+            pltpu.VMEM((n // 2, block, 2 * width), BF16),
+            pltpu.VMEM((2, block, width), BF16),
+            pltpu.VMEM((2, block, width), BF16),
+            pltpu.VMEM((2, block, width), BF16),
+            pltpu.VMEM((n // 2, block, width), BF16),
             pltpu.VMEM((slots, block, FEATURE_DIM), F32),
             pltpu.SemaphoreType.DMA((13,)),
             pltpu.SemaphoreType.DMA((n // 2,)),
             pltpu.SemaphoreType.DMA((n // 2,)),
             pltpu.SemaphoreType.DMA((n // 2 + 1,)),
+            pltpu.SemaphoreType.DMA((n // 2 + 1,)),
+            pltpu.SemaphoreType.DMA((n // 2,)),
             pltpu.SemaphoreType.DMA((n // 2 + 1,)),
             pltpu.SemaphoreType.DMA((slots,)),
             pltpu.SemaphoreType.DMA((slots,)),

time: 24 us -> 23.6 us (0.983)
  Pallas kernels: 22.3 us -> 21.9 us
    pallas_call x1, Pallas kernels: 22.3 us -> 21.9 us  [on_device(): pl.pallas_call(functools.partial(kernel, n), out_shape=pltpu.VMEM(probe_v...]
where the time goes in v3:
time: 23.6 us; the launch traced here: 23.4 us
  Pallas kernels  21.9 us (93%)
  local copies, waits for them, and re-layouts  0.85 us (4%)
  between operations  0.66 us (3%)
    pallas_call x1, Pallas kernels, on_device(): pl.pallas_call(functools.partial(kernel, n), out_shape=pltpu.VMEM(probe_v...  21.9 us
    unnamed x1, local copies, waits for them, and re-layouts  0.85 us

profile of v3, /device:TPU:0, one launch (start us, length us, event | category | flops | bytes accessed | tf_op | source)
XLA Modules:
  0.0 23.4 jit_solution(4350890381214414456)
XLA Ops:
  0.7 21.9 %shard_map.127 = bf16[6,1,32,1792]{3,2,1,0:T(8,128)(2,1)S(1)} custom-call(s32[6,1,32]{2,1,0:T(1,128)} %order_hbm.1, s32[6]{0:T(128)} %bitcast.1, s32[6,1,32]{2,1,0:T(1,128)} %choice_hbm.1, s32[1]{0:T(128)S(6)} %copy.16.index_hbm, bf16[64,256]{1,0:T(8,128)(2,1)} %noise_k_hbm.1, bf16[64,256]{1,0:T(8,128)(2,1)} %noise_v_hbm.1, bf16[6,1,32,1792]{3,2,1,0:T(8,128)(2,1)} %q_hbm.1, ...), custom_call_target="tpu_custom_call" | custom-call | tf_op jit(solution)/shard_map/pallas_call | solution.py:357
  22.6 0.8 %copy.15 = bf16[6,1,32,1792]{3,2,1,0:T(8,128)(2,1)} copy(bf16[6,1,32,1792]{3,2,1,0:T(8,128)(2,1)S(1)} %shard_map.127) | data formatting | bytes 1376256
